TPU v7x, 256 devices: a whole 4x4x8 slice. The times are simulated.
256 devices in a mesh: dp: 32 (over x, y, core), tp: 8 (over z).
Axes of the slice: x: 4, y: 4, z: 8, core: 2. Of those that a mesh axis runs over, the one named last changes fastest.
Arguments:
- tokens: bfloat16 [4096, 6144], P('dp'), may hold values from -6 to 6
- route_ids: int32 [4096, 2], P('dp'), may hold values from 0 to 3, all different within a row; in each aligned block of 128 rows (0 to 127, 128 to 255, ...) at most 72 rows name the same one
- route_weights: float32 [4096, 2], P('dp'), may hold values from 0.1 to 0.9
- grad_gate: bfloat16 [4096, 2, 8192], P('dp', None, 'tp'), may hold values from -1.1953125 to 1.1953125
- grad_up: bfloat16 [4096, 2, 8192], P('dp', None, 'tp'), may hold values from -1.1953125 to 1.1953125
- gate_weight: bfloat16 [24576, 8192], P('dp', 'tp'), may hold values from -0.078125 to 0.078125
- up_weight: bfloat16 [24576, 8192], P('dp', 'tp'), may hold values from -0.078125 to 0.078125
Outputs:
- grad_tokens: bfloat16 [4096, 6144], P('dp')
- grad_gate_weight: bfloat16 [24576, 8192], P('dp', 'tp')
- grad_up_weight: bfloat16 [24576, 8192], P('dp', 'tp')
Inputs may be any that keep to these rules, and one draw needn't show every extreme that they name: `route_ids`: in each aligned block of 128 tokens (the tokens of one index of dp), no expert is named by more than 72 of the block's routes, a bound that some block reaches; a token's 2 ids differ.
All inputs are finite; a program needn't handle non-finite values.
Results may differ from a plain program's by a relative error of at most 0.0049.
Values may be sent and summed in bfloat16 or wider, within the bound.
No kernel may reach another device: no remote copies, remote signals or barrier semaphores. Data moves between devices by JAX's collectives and lax.ppermute only.
A program may use at most 128 MiB of HBM per device.

v0:
```python
import jax
import jax.numpy as jnp
from jax import lax
from jax.sharding import PartitionSpec as P

CAP = 72


def gather_routes(rows, slot_index, tok_count, top_count):
    picked = rows[slot_index]
    return jnp.sum(picked.reshape(tok_count, top_count, -1), axis=1)


def on_device(tokens, route_ids, route_weights, grad_gate, grad_up, gate_weight, up_weight):
    dp_size = lax.axis_size("dp")
    tok_count, top_count = route_ids.shape
    width = tokens.shape[1]
    slab_cols = gate_weight.shape[0]
    hidden_cols = gate_weight.shape[1]
    groups = width // slab_cols
    experts = dp_size // groups
    capacity = CAP
    route_count = tok_count * top_count
    flat_ids = route_ids.reshape(-1)
    onehot = (flat_ids[:, None] == jnp.arange(experts, dtype=jnp.int32)[None, :]).astype(jnp.int32)
    before = jnp.cumsum(onehot, axis=0) - onehot
    position = jnp.sum(before * onehot, axis=1)
    slot_index = flat_ids * capacity + position
    source = (
        jnp.full((experts * capacity,), -1, jnp.int32)
        .at[slot_index]
        .set(jnp.arange(route_count, dtype=jnp.int32))
    )
    live_slot = source >= 0
    safe_index = jnp.maximum(source, 0)
    route_scale = route_weights.reshape(-1, 1)
    scaled_gate = (
        grad_gate.reshape(route_count, hidden_cols).astype(jnp.float32) * route_scale
    ).astype(jnp.bfloat16)
    scaled_up = (
        grad_up.reshape(route_count, hidden_cols).astype(jnp.float32) * route_scale
    ).astype(jnp.bfloat16)
    x_slots = jnp.where(
        live_slot[:, None], tokens[safe_index // top_count], jnp.zeros((), jnp.bfloat16)
    )
    x_send = (
        x_slots.reshape(experts, capacity, groups, slab_cols)
        .transpose(0, 2, 1, 3)
        .reshape(dp_size, capacity, slab_cols)
    )
    gate_slots = jnp.where(live_slot[:, None], scaled_gate[safe_index], jnp.zeros((), jnp.bfloat16))
    up_slots = jnp.where(live_slot[:, None], scaled_up[safe_index], jnp.zeros((), jnp.bfloat16))
    gate_send = jnp.broadcast_to(
        gate_slots.reshape(experts, 1, capacity, hidden_cols),
        (experts, groups, capacity, hidden_cols),
    ).reshape(dp_size, capacity, hidden_cols)
    up_send = jnp.broadcast_to(
        up_slots.reshape(experts, 1, capacity, hidden_cols),
        (experts, groups, capacity, hidden_cols),
    ).reshape(dp_size, capacity, hidden_cols)
    x_recv, gate_recv, up_recv = (
        lax.all_to_all(x_send, "dp", split_axis=0, concat_axis=0, tiled=True),
        lax.all_to_all(gate_send, "dp", split_axis=0, concat_axis=0, tiled=True),
        lax.all_to_all(up_send, "dp", split_axis=0, concat_axis=0, tiled=True),
    )
    x_rows = x_recv.reshape(dp_size * capacity, slab_cols)
    gate_rows = gate_recv.reshape(dp_size * capacity, hidden_cols)
    up_rows = up_recv.reshape(dp_size * capacity, hidden_cols)
    over_rows = (((0,), (0,)), ((), ()))
    grad_gate_weight = lax.dot_general(
        x_rows, gate_rows, over_rows, preferred_element_type=jnp.float32
    ).astype(jnp.bfloat16)
    grad_up_weight = lax.dot_general(
        x_rows, up_rows, over_rows, preferred_element_type=jnp.float32
    ).astype(jnp.bfloat16)
    over_hidden = (((1,), (1,)), ((), ()))
    partial_value = lax.dot_general(
        gate_rows, gate_weight, over_hidden, preferred_element_type=jnp.float32
    )
    partial_value = partial_value + lax.dot_general(
        up_rows, up_weight, over_hidden, preferred_element_type=jnp.float32
    )
    summed = lax.psum(partial_value, "tp")
    returned = lax.all_to_all(
        summed.reshape(dp_size, capacity, slab_cols), "dp", split_axis=0, concat_axis=0, tiled=True
    )
    pieces = (
        returned.reshape(experts, groups, capacity, slab_cols)
        .transpose(0, 2, 1, 3)
        .reshape(experts * capacity, width)
    )
    result = gather_routes(pieces, slot_index, tok_count, top_count).astype(jnp.bfloat16)
    return (result, grad_gate_weight, grad_up_weight)


def solution(mesh):
    return jax.shard_map(
        on_device,
        mesh=mesh,
        in_specs=(
            P("dp", None),
            P("dp", None),
            P("dp", None),
            P("dp", None, "tp"),
            P("dp", None, "tp"),
            P("dp", "tp"),
            P("dp", "tp"),
        ),
        out_specs=(P("dp", None), P("dp", "tp"), P("dp", "tp")),
        check_vma=False,
    )
```

profile of v0, /device:TPU:12, one launch (start us, length us, event | category | flops | bytes accessed | tf_op | source)
XLA Modules:
  0.0 494.5 jit_solution(2908125160368990511)
XLA Ops:
  7.2 0.0 copy-start
  7.2 0.8 broadcast_multiply_fusion
  8.0 0.8 copy.15
  8.8 0.1 eq.29
  8.9 0.1 eq.25
  9.0 0.1 copy.14
  9.2 0.1 mul.37
  9.3 1.2 reduce-window.6
  10.5 0.1 slice.16
  10.6 0.1 copy.17
  10.8 0.1 copy.18
  10.9 0.1 add_bitcast_fusion
  11.0 1.4 scatter_custom_fusion
  12.4 0.1 broadcast_in_dim.57
  12.5 0.8 copy.19
  13.3 0.1 mul.39
  13.4 2.2 reshape.130
  15.6 2.2 reshape.131
  17.7 1.7 multiply_convert_fusion
  19.5 2.1 gather_fusion.1
  21.6 2.6 gather_fusion
  24.2 1.2 broadcast_select_fusion
  25.4 0.6 broadcast_in_dim.61
  26.0 60.8 %all_to_all.20 = bf16[32,72,1024]{2,1,0:T(8,128)(2,1)} all-to-all(bf16[32,72,1024]{2,1,0:T(8,128)(2,1)S(1)} %bitcast.55), channel_id=1, replica_groups=mesh['dp'=32,'tp'=8] {'dp'}, dimensions={0} | all-to-all | bytes 9437184 | tf_op jit(solution)/shard_map/all_to_all | solution.py:63
  86.8 2.7 broadcast_in_dim.62
  89.5 7.5 %all-to-all-start.1 = ((bf16[32,72,1024]{2,1,0:T(8,128)(2,1)}), bf16[32,72,1024]{2,1,0:T(8,128)(2,1)}, u32[]{:S(2)}, u32[]{:S(2)}) async-start(bf16[32,72,1024]{2,1,0:T(8,128)(2,1)} %bitcast.54), calls=%async_computation.1 | async-start | bytes 9437184 | tf_op jit(solution)/shard_map/all_to_all | solution.py:64
  97.0 0.0 all-reduce.2.cloned.1.call-start
  97.1 0.0 copy-done
  97.1 0.0 copy-start.4
  97.1 8.3 %fusion.6 = f32[2304,768]{1,0:T(8,128)} fusion(bf16[2304,1024]{1,0:T(8,128)(2,1)} %bitcast.60, bf16[768,1024]{1,0:T(8,128)(2,1)S(1)} %copy-done), kind=kOutput, calls=%fused_computation.34 | convolution fusion | flops 3623878656 | bytes 13369344 | tf_op jit(solution)/shard_map/dot_general | solution.py:77
  105.3 51.3 %all-to-all-done.1 = bf16[32,72,1024]{2,1,0:T(8,128)(2,1)} async-done(((bf16[32,72,1024]{2,1,0:T(8,128)(2,1)}), bf16[32,72,1024]{2,1,0:T(8,128)(2,1)}, u32[]{:S(2)}, u32[]{:S(2)}) %all-to-all-start.1) | async-done | bytes 4718624 | tf_op jit(solution)/shard_map/all_to_all | solution.py:64
  156.6 0.0 copy-done.4
  156.6 10.2 %convolution_add_fusion = f32[2304,768]{1,0:T(8,128)} fusion(f32[2304,768]{1,0:T(8,128)} %fusion.6, bf16[2304,1024]{1,0:T(8,128)(2,1)} %bitcast.9, bf16[768,1024]{1,0:T(8,128)(2,1)S(1)} %copy-done.4), kind=kOutput, calls=%fused_computation.5 | convolution fusion | flops 3625648128 | bytes 20447232 | tf_op jit(solution)/shard_map/dot_general | solution.py:80
  166.8 0.0 copy-start.2
  166.8 0.0 all-reduce.2.cloned.1.call-update
  166.9 1.4 copy-done.2
  168.3 5.1 %gather_fusion.3 = bf16[288,6144]{1,0:T(8,128)(2,1)} fusion(bf16[128,6144]{1,0:T(8,128)(2,1)S(1)} %copy-done.2, s32[1024]{0:T(1024)S(1)} %get-tuple-element.9), kind=kCustom, calls=%fused_computation.3 | custom fusion | bytes 7079040 | tf_op jit(solution)/shard_map/gather | solution.py:44
  173.4 3.0 copy.24
  176.4 0.7 copy_select_fusion
  177.1 48.0 %all_to_all.21 = bf16[32,72,768]{2,1,0:T(8,128)(2,1)} all-to-all(bf16[32,72,768]{2,1,0:T(8,128)(2,1)S(1)} %bitcast.57), channel_id=1, replica_groups=mesh['dp'=32,'tp'=8] {'dp'}, dimensions={0} | all-to-all | bytes 7077888 | tf_op jit(solution)/shard_map/all_to_all | solution.py:62
  225.1 107.5 %all-reduce.2.cloned.1.call-done = f32[32,72,768]{2,1,0:T(8,128)} async-done(((f32[32,72,768]{2,1,0:T(8,128)}), f32[32,72,768]{2,1,0:T(8,128)}) %all-reduce.2.cloned.1.call-update) | async-done | bytes 7077904 | tf_op jit(solution)/shard_map/psum | solution.py:83
  332.6 0.0 slice-start
  332.6 7.6 %all-to-all-start.2 = ((f32[32,72,768]{2,1,0:T(8,128)}), f32[32,72,768]{2,1,0:T(8,128)}, u32[]{:S(2)}, u32[]{:S(2)}) async-start(f32[32,72,768]{2,1,0:T(8,128)} %all-reduce.2.cloned.1.call-done), calls=%async_computation.2 | async-start | bytes 14155776 | tf_op jit(solution)/shard_map/all_to_all | solution.py:84
  340.2 0.0 slice-start.1
  340.2 0.0 copy-start.3
  340.2 8.6 %bitcast_convert_fusion = bf16[768,1024]{1,0:T(8,128)(2,1)} fusion(bf16[32,72,768]{2,1,0:T(8,128)(2,1)} %all_to_all.21, bf16[32,72,1024]{2,1,0:T(8,128)(2,1)} %all-to-all-done.1), kind=kOutput, calls=%fused_computation.7 | convolution fusion | flops 3624665088 | bytes 9830400 | tf_op jit(solution)/shard_map/dot_general | solution.py:73
  348.8 0.0 slice-done
  348.8 0.0 slice-done.1
  348.8 0.0 copy-done.3
  348.8 5.0 %bitcast_convert_fusion.1 = bf16[768,1024]{1,0:T(8,128)(2,1)} fusion(bf16[32,72,768]{2,1,0:T(8,128)(2,1)S(1)} %copy-done.3, bf16[32,72,1024]{2,1,0:T(8,128)(2,1)S(1)} %bitcast.62), kind=kOutput, calls=%fused_computation.8 | convolution fusion | flops 3624665088 | bytes 9830400 | tf_op jit(solution)/shard_map/dot_general | solution.py:70
  353.8 91.6 %all-to-all-done.2 = f32[32,72,768]{2,1,0:T(8,128)} async-done(((f32[32,72,768]{2,1,0:T(8,128)}), f32[32,72,768]{2,1,0:T(8,128)}, u32[]{:S(2)}, u32[]{:S(2)}) %all-to-all-start.2) | async-done | bytes 7077920 | tf_op jit(solution)/shard_map/all_to_all | solution.py:84
  445.4 5.2 %copy.20 = f32[4,8,72,768]{3,1,2,0:T(8,128)S(1)} copy(f32[4,8,72,768]{3,2,1,0:T(8,128)} %bitcast.11) | data formatting | bytes 14155776 | tf_op jit(solution)/shard_map/reshape | solution.py:88
  450.5 5.9 %copy.23 = f32[36,8,8,768]{3,1,2,0:T(8,128)} copy(f32[36,8,8,768]{3,2,1,0:T(8,128)S(1)} %bitcast.53) | data formatting | bytes 14155776
  456.4 10.9 %gather_fusion.2 = f32[256,6144]{1,0:T(8,128)} fusion(f32[288,6144]{1,0:T(8,128)} %bitcast.52, s32[1024]{0:T(1024)S(1)} %pad_clamp_fusion.1), kind=kCustom, calls=%fused_computation.2 | custom fusion | bytes 12583936 | tf_op jit(solution)/shard_map/gather | solution.py:10
  467.3 0.0 copy-start.1
  467.3 8.4 %reshape.128 = f32[128,2,6144]{2,1,0:T(2,128)} reshape(f32[256,6144]{1,0:T(8,128)} %gather_fusion.2) | data formatting | bytes 12582912 | tf_op jit(solution)/shard_map/reshape | solution.py:11
  475.7 11.7 %reduce_sum.22 = bf16[128,6144]{1,0:T(8,128)(2,1)} reduce(f32[128,2,6144]{2,1,0:T(2,128)} %reshape.128, f32[]{:T(128)} %constant.33.clone.1), dimensions={1}, to_apply=%region_5.6 | reduce | flops 786432 | bytes 7864324 | tf_op jit(solution)/shard_map/reduce_sum | solution.py:11
  487.4 0.0 copy-done.1
  (11 shorter events, 0.1 us)
Async XLA Ops:
  7.2 89.9 %copy-start = (bf16[768,1024]{1,0:T(8,128)(2,1)S(1)}, bf16[768,1024]{1,0:T(8,128)(2,1)}, u32[]{:S(2)}) copy-start(bf16[768,1024]{1,0:T(8,128)(2,1)} %param.12) | copy-start | bytes 4718596
  89.5 67.1 %all-to-all-start.1 = ((bf16[32,72,1024]{2,1,0:T(8,128)(2,1)}), bf16[32,72,1024]{2,1,0:T(8,128)(2,1)}, u32[]{:S(2)}, u32[]{:S(2)}) async-start(bf16[32,72,1024]{2,1,0:T(8,128)(2,1)} %bitcast.54), calls=%async_computation.1 | async-start | bytes 9437184 | tf_op jit(solution)/shard_map/all_to_all | solution.py:64
  97.0 235.6 %all-reduce.2.cloned.1.call-start = ((), (), s32[]{:S(2)}) async-start(), calls=%async_computation.4 | async-start | bytes 14155776 | tf_op jit(solution)/shard_map/psum | solution.py:83
  97.1 59.5 %copy-start.4 = (bf16[768,1024]{1,0:T(8,128)(2,1)S(1)}, bf16[768,1024]{1,0:T(8,128)(2,1)}, u32[]{:S(2)}) copy-start(bf16[768,1024]{1,0:T(8,128)(2,1)} %param.13) | copy-start | bytes 4718596
  166.8 1.4 copy-start.2
  332.6 16.2 %slice-start = ((s8[4718592]{0:T(1024)(128)(4,1)}), s8[524288]{0:T(1024)(128)(4,1)S(1)}, s32[]{:S(2)}) async-start(s8[4718592]{0:T(1024)(128)(4,1)} %bitcast.61), calls=%async_computation.5 | async-start | bytes 1048576
  332.6 112.8 %all-to-all-start.2 = ((f32[32,72,768]{2,1,0:T(8,128)}), f32[32,72,768]{2,1,0:T(8,128)}, u32[]{:S(2)}, u32[]{:S(2)}) async-start(f32[32,72,768]{2,1,0:T(8,128)} %all-reduce.2.cloned.1.call-done), calls=%async_computation.2 | async-start | bytes 14155776 | tf_op jit(solution)/shard_map/all_to_all | solution.py:84
  340.2 8.6 %slice-start.1 = ((s8[4718592]{0:T(1024)(128)(4,1)}), s8[4194304]{0:T(1024)(128)(4,1)S(1)}, s32[]{:S(2)}) async-start(s8[4718592]{0:T(1024)(128)(4,1)} %bitcast.61), calls=%async_computation.6 | async-start | bytes 8388608
  340.2 8.6 %copy-start.3 = (bf16[32,72,768]{2,1,0:T(8,128)(2,1)S(1)}, bf16[32,72,768]{2,1,0:T(8,128)(2,1)}, u32[]{:S(2)}) copy-start(bf16[32,72,768]{2,1,0:T(8,128)(2,1)} %all_to_all.21) | copy-start | bytes 10616836
  467.3 20.1 %copy-start.1 = (bf16[768,1024]{1,0:T(8,128)(2,1)S(1)}, bf16[768,1024]{1,0:T(8,128)(2,1)}, u32[]{:S(2)}) copy-start(bf16[768,1024]{1,0:T(8,128)(2,1)} %param.12) | copy-start | bytes 4718596
Sparse Core Ops, SparseCore 0:
  167.0 165.5 all-reduce.1
where the time goes:
time: 504 us; the launch traced here: 494 us
  waiting for transfers between devices  250 us (50%)
  blocking collectives  109 us (22%)
  local copies, waits for them, and re-layouts  56.3 us (11%)
  matrix products  32 us (6%)
  other arithmetic  17.5 us (3%)
  starting transfers between devices  15.1 us (3%)
  between operations  14.4 us (3%)
    psum x1, waiting for transfers between devices, on_device(): summed = lax.psum(partial_value, 'tp')  107 us
    all_to_all x1, waiting for transfers between devices, on_device(): lax.all_to_all(summed.reshape(dp_size, capacity, slab_cols), 'dp', split_...  91.6 us
    all_to_all x1, blocking collectives, on_device(): lax.all_to_all(gate_send, 'dp', split_axis=0, concat_axis=0, tiled=True)  60.8 us
    all_to_all x1, waiting for transfers between devices, on_device(): lax.all_to_all(up_send, 'dp', split_axis=0, concat_axis=0, tiled=True)  51.3 us
    all_to_all x1, blocking collectives, on_device(): lax.all_to_all(x_send, 'dp', split_axis=0, concat_axis=0, tiled=True)  48 us
    unnamed x18, local copies, waits for them, and re-layouts  11.9 us
    reduce_sum x1, other arithmetic, gather_routes(): return jnp.sum(picked.reshape(tok_count, top_count, -1), axis=1)  11.7 us
    gather x1, local copies, waits for them, and re-layouts, gather_routes(): picked = rows[slot_index]  10.9 us
  transfers between devices with their start and end apart: 3, of which 3 were waited for; matrix products, arithmetic and copies ran while one was open for 6% of the time, Pallas kernels for 0%

commit v1 on v0

v1 whole, which is shorter than its diff:
```python
import jax
import jax.numpy as jnp
from jax import lax
from jax.experimental import pallas as pl
from jax.experimental.pallas import tpu as pltpu
from jax.sharding import PartitionSpec as P

CAP = 72
NX, NY, NC, NZ = 4, 4, 2, 8
BF, F32, I32 = jnp.bfloat16, jnp.float32, jnp.int32
VM = pl.BlockSpec(memory_space=pltpu.VMEM)
SM = pl.BlockSpec(memory_space=pltpu.SMEM)
ANY = pl.BlockSpec(memory_space=pl.ANY)
LIMIT = 48 * 1024 * 1024


def dp_perm(move):
    pairs = []
    for x in range(NX):
        for y in range(NY):
            for c in range(NC):
                tx, ty, tc = move(x, y, c)
                pairs.append(((x * NY + y) * NC + c, (tx % NX * NY + ty % NY) * NC + tc % NC))
    return pairs


def x_shift(value, k):
    return lax.ppermute(value, "dp", dp_perm(lambda x, y, c: (x + k, y, c)))


def y_shift(value, k):
    return lax.ppermute(value, "dp", dp_perm(lambda x, y, c: (x, y + k, c)))


def c_swap(value):
    return lax.ppermute(value, "dp", dp_perm(lambda x, y, c: (x, y, c + 1)))


def z_shift(value, k):
    return lax.ppermute(value, "tp", [(i, (i + k) % NZ) for i in range(NZ)])


def swap_low_z(value):
    pairs = []
    for x in range(NX):
        for low in range(NY * NC):
            for z in range(NZ):
                pairs.append(((x * 8 + low) * NZ + z, (x * 8 + z) * NZ + low))
    return lax.ppermute(value, ("dp", "tp"), pairs)


def one_hot_slots(ids):
    n = ids.shape[1]
    tri = (
        lax.broadcasted_iota(I32, (n, n), 0) < lax.broadcasted_iota(I32, (n, n), 1)
    ).astype(F32).astype(BF)
    rank = lax.broadcasted_iota(I32, (8, n), 0)
    hot0 = (rank == ids[0:1, :]).astype(F32)
    hot1 = (rank == ids[1:2, :]).astype(F32)
    pos0 = jnp.dot(hot0.astype(BF), tri, preferred_element_type=F32)
    pos1 = jnp.dot(hot1.astype(BF), tri, preferred_element_type=F32)
    pos1 = pos1 + jnp.sum(hot0, axis=1, keepdims=True)
    slot = lax.broadcasted_iota(I32, (CAP, n), 0)
    pairs = []
    for e in range(NX):
        at0 = jnp.where(hot0[e : e + 1, :] > 0.5, pos0[e : e + 1, :], -1.0).astype(I32)
        at1 = jnp.where(hot1[e : e + 1, :] > 0.5, pos1[e : e + 1, :], -1.0).astype(I32)
        pairs.append(((slot == at0).astype(F32), (slot == at1).astype(F32)))
    return pairs


def dispatch_kernel(ids_ref, w_ref, gg_ref, gu_ref, *out_refs):
    hots = one_hot_slots(ids_ref[...])
    w = w_ref[...]
    ff = gg_ref.shape[2]
    for part, ref in enumerate((gg_ref, gu_ref)):
        s0 = (ref[:, 0, :].astype(F32) * w[:, 0:1]).astype(BF)
        s1 = (ref[:, 1, :].astype(F32) * w[:, 1:2]).astype(BF)
        for e in range(NX):
            d0, d1 = hots[e]
            rows = jnp.dot(d0.astype(BF), s0, preferred_element_type=F32)
            rows = rows + jnp.dot(d1.astype(BF), s1, preferred_element_type=F32)
            out_refs[e][:, part * ff : (part + 1) * ff] = rows.astype(BF)


def token_kernel(x_ref, ids_ref, tok_ref, dep_ref, out_ref):
    hots = one_hot_slots(ids_ref[...])
    slabs = NY * NC
    cols = tok_ref.shape[1] // slabs
    for k in range(NX):
        d = (hots[k][0] + hots[k][1]).astype(BF)
        base = lax.rem(x_ref[0] + k, NX) * slabs
        for g in range(slabs):
            rows = jnp.dot(d, tok_ref[:, g * cols : (g + 1) * cols], preferred_element_type=F32)
            out_ref[base + g] = rows.astype(BF)


def partial_kernel(o_ref, g_ref, u_ref, *refs):
    pieces, (p_ref, s_ref) = refs[:-2], refs[-2:]
    ff = g_ref.shape[1]
    cols = g_ref.shape[0]
    over = (((1,), (1,)), ((), ()))
    at = 0
    n = 4 * CAP
    for ref in pieces:
        s_ref[at : at + ref.shape[0], :] = ref[...]
        at += ref.shape[0]
    tile = 256
    for m in range(8):
        slot = o_ref[m]

        def step(t, _, m=m, slot=slot):
            c = pl.multiple_of(t * tile, tile)
            acc = lax.dot_general(
                s_ref[m * n : (m + 1) * n, 0:ff], g_ref[pl.ds(c, tile), :], over, preferred_element_type=F32
            )
            acc = acc + lax.dot_general(
                s_ref[m * n : (m + 1) * n, ff : 2 * ff], u_ref[pl.ds(c, tile), :], over, preferred_element_type=F32
            )
            p_ref[slot, :, pl.ds(c, tile)] = acc.astype(BF)
            return 0

        lax.fori_loop(0, cols // tile, step, 0)


def combine_kernel(ids_ref, *refs):
    pieces, out_ref = refs[:-1], refs[-1]
    hots = one_hot_slots(ids_ref[...])
    over = (((0,), (0,)), ((), ()))
    total = None
    for k in range(NX):
        d = (hots[k][0] + hots[k][1]).astype(BF)
        part = lax.dot_general(d, pieces[k][...], over, preferred_element_type=F32)
        total = part if total is None else total + part
    out_ref[...] = total.astype(BF)


def assemble_kernel(slab_ref, *refs):
    pieces, out_ref = refs[:-1], refs[-1]
    cols = pieces[0].shape[1]
    for i, ref in enumerate(pieces):
        at = pl.multiple_of(slab_ref[i] * cols, 128)
        out_ref[:, pl.ds(at, cols)] = ref[...]


def call(kernel, out_shape, in_specs, flops=0, nbytes=0):
    return pl.pallas_call(
        kernel,
        out_shape=out_shape,
        in_specs=in_specs,
        out_specs=jax.tree.map(lambda _: VM, out_shape),
        compiler_params=pltpu.CompilerParams(vmem_limit_bytes=LIMIT),
        cost_estimate=pl.CostEstimate(flops=flops, bytes_accessed=nbytes, transcendentals=0),
    )


def on_device(tokens, route_ids, route_weights, grad_gate, grad_up, gate_weight, up_weight):
    toks, width = tokens.shape
    cols, ff = gate_weight.shape
    dp, z = lax.axis_index("dp"), lax.axis_index("tp")
    x, y, c = dp // 8, dp // 2 % 4, dp % 2
    ids = lax.rem(route_ids.T - x + NX, NX)
    ids_back = swap_low_z(ids)
    sent = call(
        dispatch_kernel,
        [jax.ShapeDtypeStruct((CAP, 2 * ff), BF)] * NX,
        [VM] * 4,
        2 * NX * CAP * toks * 2 * 2 * ff,
        4 << 20,
    )(ids, route_weights, grad_gate, grad_up)
    own = jnp.concatenate([sent[0]] + [x_shift(sent[k], k) for k in range(1, NX)], axis=0)
    half = 2 * CAP
    up1, down1 = y_shift(own, 1), y_shift(own, -1)
    up2, down2 = y_shift(up1[:half], 1), y_shift(down1[half:], -1)
    pieces = [own, up1, down1, up2, down2]
    pieces = pieces + [c_swap(p) for p in pieces]
    places = [(0, 0), (3, 0), (1, 0), (2, 0), (0, 1), (3, 1), (1, 1), (2, 1)]
    low = jnp.stack([(y + j) % NY * NC + (c + i) % NC for j, i in places]).astype(I32)
    offset = lax.rem(low - z + NZ, NZ)
    chunks, s_all = call(
        partial_kernel,
        [jax.ShapeDtypeStruct((8, 4 * CAP, cols), BF), jax.ShapeDtypeStruct((32 * CAP, 2 * ff), BF)],
        [SM] + [VM] * 12,
        2 * 32 * CAP * 2 * ff * cols,
        24 << 20,
    )(offset, gate_weight, up_weight, *pieces)

    up, down = chunks[4], chunks[5]
    for o in (3, 2, 1):
        up = z_shift(up, 1)
        up = (up.astype(F32) + chunks[o].astype(F32)).astype(BF)
        if o > 1:
            down = z_shift(down, -1)
            down = (down.astype(F32) + chunks[9 - o].astype(F32)).astype(BF)
    up, down = z_shift(up, 1), z_shift(down, -1)
    summed = (up.astype(F32) + down.astype(F32) + chunks[0].astype(F32)).astype(BF)
    back = [x_shift(summed[k * CAP : (k + 1) * CAP], -k) if k else summed[:CAP] for k in range(NX)]
    mine = call(
        combine_kernel, jax.ShapeDtypeStruct((toks, cols), BF), [VM] * 5, 2 * NX * CAP * toks * cols, 1 << 20
    )(ids_back, *back)
    mine = swap_low_z(mine)
    parts, up, down = [mine], mine, mine
    for step in range(4):
        up = z_shift(up, 1)
        parts.append(up)
        if step < 3:
            down = z_shift(down, -1)
            parts.append(down)
    slab = jnp.stack([(z + d) % NZ for d in (0, -1, 1, -2, 2, -3, 3, -4)]).astype(I32)
    result = call(
        assemble_kernel, jax.ShapeDtypeStruct((toks, width), BF), [SM] + [VM] * 8, 0, 3 << 20
    )(slab, *parts)

    x_send = call(
        token_kernel,
        jax.ShapeDtypeStruct((32, CAP, cols), BF),
        [SM, VM, VM, ANY],
        2 * NX * CAP * toks * width,
        5 << 20,
    )(x.reshape(1).astype(I32), ids, tokens, pieces[3])
    x_recv = lax.all_to_all(x_send, "dp", split_axis=0, concat_axis=0, tiled=True)
    order = jnp.stack(
        [(x - k) % NX * 8 + low[m] for m in range(8) for k in range(NX)]
    ).astype(I32)
    x_rows = x_recv[order].reshape(32 * CAP, cols)
    over_rows = (((0,), (0,)), ((), ()))
    grad_gate_weight = lax.dot_general(
        x_rows, s_all[:, :ff], over_rows, preferred_element_type=F32
    ).astype(BF)
    grad_up_weight = lax.dot_general(
        x_rows, s_all[:, ff:], over_rows, preferred_element_type=F32
    ).astype(BF)
    return (result, grad_gate_weight, grad_up_weight)


def solution(mesh):
    return jax.shard_map(
        on_device,
        mesh=mesh,
        in_specs=(
            P("dp", None),
            P("dp", None),
            P("dp", None),
            P("dp", None, "tp"),
            P("dp", None, "tp"),
            P("dp", "tp"),
            P("dp", "tp"),
        ),
        out_specs=(P("dp", None), P("dp", "tp"), P("dp", "tp")),
        check_vma=False,
    )
```

time: 504 us -> 238 us (0.47)
  the two profiles are of different devices: /device:TPU:12 before, /device:TPU:6 now
where the time goes in v1:
time: 238 us
  waiting for transfers between devices  110 us (46%)
  starting transfers between devices  66.2 us (28%)
  Pallas kernels  27.3 us (11%)
  matrix products  15.9 us (7%)
  local copies, waits for them, and re-layouts  12.1 us (5%)
  other arithmetic  5.7 us (2%)
    ppermute x14, waiting for transfers between devices, z_shift(): return lax.ppermute(value, 'tp', [(i, (i + k) % NZ) for i in range(NZ)])  46.5 us
    ppermute x14, starting transfers between devices, z_shift(): return lax.ppermute(value, 'tp', [(i, (i + k) % NZ) for i in range(NZ)])  42.2 us
    ppermute x4, waiting for transfers between devices, y_shift(): return lax.ppermute(value, 'dp', dp_perm(lambda x, y, c: (x, y + k, c)))  39.1 us
    ppermute x6, waiting for transfers between devices, x_shift(): return lax.ppermute(value, 'dp', dp_perm(lambda x, y, c: (x + k, y, c)))  22 us
    pallas_call x1, Pallas kernels, on_device(): call(partial_kernel, [jax.ShapeDtypeStruct((8, 4 * CAP, cols), BF), jax.S...  20.5 us
    dot_general x1, matrix products, on_device(): lax.dot_general(x_rows, s_all[:, :ff], over_rows, preferred_element_type=...  8.56 us
    all_to_all x1, starting transfers between devices, on_device(): lax.all_to_all(x_send, 'dp', split_axis=0, concat_axis=0, tiled=True)  7.89 us
    ppermute x6, starting transfers between devices, x_shift(): return lax.ppermute(value, 'dp', dp_perm(lambda x, y, c: (x + k, y, c)))  7.69 us
  transfers between devices with their start and end apart: 32, of which 18 were waited for; matrix products, arithmetic and copies ran while one was open for 12% of the time, Pallas kernels for 2%

profile of v1, /device:TPU:6, one launch (start us, length us, event | category | flops | bytes accessed | tf_op | source)
XLA Modules:
  0.0 237.6 jit_solution(6950659256749761148)
XLA Ops:
  0.6 0.8 copy.10.w_ref
  1.4 0.7 compare_select_fusion.3.ids_ref
  2.1 1.0 copy-done.1
  3.2 1.0 copy-done.2
  4.2 1.4 shard_map.94
  5.7 2.3 collective-permute-start.1
  7.9 0.7 collective-permute-start.2
  8.6 0.3 collective-permute-start.3
  8.9 0.7 constant_dynamic-update-slice_fusion.3
  9.6 6.0 %collective-permute-done.1 = bf16[72,2048]{1,0:T(8,128)(2,1)S(1)} collective-permute-done((bf16[72,2048]{1,0:T(8,128)(2,1)S(1)}, bf16[72,2048]{1,0:T(8,128)(2,1)S(1)}, u32[]{:S(2)}, u32[]{:S(2)}) %collective-permute-start.1) | collective-permute-done | bytes 294944 | tf_op jit(solution)/shard_map/ppermute | solution.py:28
  15.6 0.7 constant_dynamic-update-slice_fusion.2
  16.4 2.9 %collective-permute-done.2 = bf16[72,2048]{1,0:T(8,128)(2,1)S(1)} collective-permute-done((bf16[72,2048]{1,0:T(8,128)(2,1)S(1)}, bf16[72,2048]{1,0:T(8,128)(2,1)S(1)}, u32[]{:S(2)}, u32[]{:S(2)}) %collective-permute-start.2) | collective-permute-done | bytes 294944 | tf_op jit(solution)/shard_map/ppermute | solution.py:28
  19.3 0.7 constant_dynamic-update-slice_fusion.1
  20.0 2.4 %collective-permute-done.3 = bf16[72,2048]{1,0:T(8,128)(2,1)S(1)} collective-permute-done((bf16[72,2048]{1,0:T(8,128)(2,1)S(1)}, bf16[72,2048]{1,0:T(8,128)(2,1)S(1)}, u32[]{:S(2)}, u32[]{:S(2)}) %collective-permute-start.3) | collective-permute-done | bytes 294944 | tf_op jit(solution)/shard_map/ppermute | solution.py:28
  22.4 0.7 constant_dynamic-update-slice_fusion.refs_0_
  23.1 1.7 collective-permute-start.4
  24.8 1.6 collective-permute-start.5
  26.4 26.2 %collective-permute-done.4.refs_1_ = bf16[288,2048]{1,0:T(8,128)(2,1)S(1)} collective-permute-done((bf16[288,2048]{1,0:T(8,128)(2,1)}, bf16[288,2048]{1,0:T(8,128)(2,1)S(1)}, u32[]{:S(2)}, u32[]{:S(2)}) %collective-permute-start.4) | collective-permute-done | bytes 1179680 | tf_op jit(solution)/shard_map/ppermute | solution.py:32
  52.7 0.4 collective-permute-start.6
  53.1 0.6 collective-permute-start.10
  53.7 2.9 %collective-permute-start.7 = (bf16[144,2048]{1,0:T(8,128)(2,1)S(1)}, bf16[144,2048]{1,0:T(8,128)(2,1)S(1)}, u32[]{:S(2)}, u32[]{:S(2)}) collective-permute-start(bf16[144,2048]{1,0:T(8,128)(2,1)S(1)} %slice.67), channel_id=1, source_target_pairs={{0,48},{8,56},{16,0},{24,8},{32,16},{40,24},{48,32},{56,40},{64,11... | collective-permute-start | bytes 1769480 | tf_op jit(solution)/shard_map/ppermute | solution.py:32
  56.6 11.9 %collective-permute-done.6.refs_3_.dep_ref = bf16[144,2048]{1,0:T(8,128)(2,1)S(1)} collective-permute-done((bf16[144,2048]{1,0:T(8,128)(2,1)S(1)}, bf16[144,2048]{1,0:T(8,128)(2,1)S(1)}, u32[]{:S(2)}, u32[]{:S(2)}) %collective-permute-start.6) | collective-permute-done | bytes 589856 | tf_op jit(solution)/shard_map/ppermute | solution.py:32
  68.5 0.9 collective-permute-done.7.refs_4_
  69.5 0.1 stack.170
  69.6 1.1 collective-permute-done.11.refs_8_
  70.7 0.9 collective-permute-done.12.refs_9_
  71.6 20.5 %shard_map.95 = (bf16[8,288,768]{2,1,0:T(8,128)(2,1)}, bf16[2304,2048]{1,0:T(8,128)(2,1)}) custom-call(s32[8]{0:T(128)S(1)} %compare_select_fusion.1.o_ref, bf16[768,1024]{1,0:T(8,128)(2,1)} %g_ref.1, bf16[768,1024]{1,0:T(8,128)(2,1)} %u_ref.1, bf16[288,2048]{1,0:T(8,128)(2,1)} %constant_dynamic-update-slice_fusion.refs_0_, ...), custom_call_target="tpu_custom_call" | custom-call | flops 7247757312 | bytes 25165824 | tf_op jit(solution)/shard_map/pallas_call | solution.py:180
  92.1 1.3 slice_bitcast_fusion.1
  93.4 2.0 collective-permute-start.13
  95.4 4.0 %collective-permute-start.17 = (bf16[288,768]{1,0:T(8,128)(2,1)S(1)}, bf16[288,768]{1,0:T(8,128)(2,1)S(1)}, u32[]{:S(2)}, u32[]{:S(2)}) collective-permute-start(bf16[288,768]{1,0:T(8,128)(2,1)S(1)} %get-tuple-element.20), channel_id=1, source_target_pairs={{0,7},{1,0},{2,1},{3,2},{4,3},{5,4},{6,5},{7,6},{8,15},{9,8},{10,9... | collective-permute-start | bytes 1327112 | tf_op jit(solution)/shard_map/ppermute | solution.py:40
  99.4 10.4 %collective-permute-done.13 = bf16[288,768]{1,0:T(8,128)(2,1)S(1)} collective-permute-done((bf16[288,768]{1,0:T(8,128)(2,1)S(1)}, bf16[288,768]{1,0:T(8,128)(2,1)S(1)}, u32[]{:S(2)}, u32[]{:S(2)}) %collective-permute-start.13) | collective-permute-done | bytes 442400 | tf_op jit(solution)/shard_map/ppermute | solution.py:40
  109.8 1.1 fusion.15
  111.0 3.1 %shard_map.98 = bf16[32,72,768]{2,1,0:T(8,128)(2,1)} custom-call(s32[1]{0:T(128)} %bitcast.25.x_ref, s32[2,128]{1,0:T(2,128)S(1)} %compare_select_fusion.3.ids_ref, bf16[128,6144]{1,0:T(8,128)(2,1)S(1)} %copy-done, bf16[144,2048]{1,0:T(8,128)(2,1)S(1)} %collective-permute-done.6.refs_3_.dep_ref), custom_call_target="tpu_custom_call" | custom-call | flops 452984832 | bytes 5242880 | tf_op jit(solution)/shard_map/pallas_call | solution.py:214
  114.1 7.9 %all-to-all-start = ((bf16[32,72,768]{2,1,0:T(8,128)(2,1)}), bf16[32,72,768]{2,1,0:T(8,128)(2,1)}, u32[]{:S(2)}, u32[]{:S(2)}) async-start(bf16[32,72,768]{2,1,0:T(8,128)(2,1)} %shard_map.98), calls=%async_computation | async-start | bytes 7077888 | tf_op jit(solution)/shard_map/all_to_all | solution.py:221
  122.0 1.9 collective-permute-done.14
  123.9 1.4 fusion.14
  125.4 3.2 %collective-permute-start.18 = (bf16[288,768]{1,0:T(8,128)(2,1)S(1)}, bf16[288,768]{1,0:T(8,128)(2,1)S(1)}, u32[]{:S(2)}, u32[]{:S(2)}) collective-permute-start(bf16[288,768]{1,0:T(8,128)(2,1)S(1)} %get-tuple-element.18), channel_id=1, source_target_pairs={{0,7},{1,0},{2,1},{3,2},{4,3},{5,4},{6,5},{7,6},{8,15},{9,8},{10,9... | collective-permute-start | bytes 1327112 | tf_op jit(solution)/shard_map/ppermute | solution.py:40
  128.6 8.8 %collective-permute-done.15 = bf16[288,768]{1,0:T(8,128)(2,1)S(1)} collective-permute-done((bf16[288,768]{1,0:T(8,128)(2,1)S(1)}, bf16[288,768]{1,0:T(8,128)(2,1)S(1)}, u32[]{:S(2)}, u32[]{:S(2)}) %collective-permute-start.15) | collective-permute-done | bytes 442400 | tf_op jit(solution)/shard_map/ppermute | solution.py:40
  137.4 1.4 fusion.13
  138.7 3.0 %collective-permute-start.19 = (bf16[288,768]{1,0:T(8,128)(2,1)S(1)}, bf16[288,768]{1,0:T(8,128)(2,1)S(1)}, u32[]{:S(2)}, u32[]{:S(2)}) collective-permute-start(bf16[288,768]{1,0:T(8,128)(2,1)S(1)} %get-tuple-element.16), channel_id=1, source_target_pairs={{0,7},{1,0},{2,1},{3,2},{4,3},{5,4},{6,5},{7,6},{8,15},{9,8},{10,9... | collective-permute-start | bytes 1327112 | tf_op jit(solution)/shard_map/ppermute | solution.py:40
  141.7 9.0 %collective-permute-done.19 = bf16[288,768]{1,0:T(8,128)(2,1)S(1)} collective-permute-done((bf16[288,768]{1,0:T(8,128)(2,1)S(1)}, bf16[288,768]{1,0:T(8,128)(2,1)S(1)}, u32[]{:S(2)}, u32[]{:S(2)}) %collective-permute-start.19) | collective-permute-done | bytes 442400 | tf_op jit(solution)/shard_map/ppermute | solution.py:40
  150.8 2.0 collective-permute-done.16
  152.7 1.2 fusion.10
  154.0 1.7 collective-permute-start.20
  155.6 0.5 collective-permute-start.21
  156.1 2.3 collective-permute-start.22
  158.4 0.6 collective-permute-start
  159.1 5.0 %collective-permute-done.20.refs_1_ = bf16[72,768]{1,0:T(8,128)(2,1)S(1)} collective-permute-done((bf16[72,768]{1,0:T(8,128)(2,1)S(1)}, bf16[72,768]{1,0:T(8,128)(2,1)S(1)}, u32[]{:S(2)}, u32[]{:S(2)}) %collective-permute-start.20) | collective-permute-done | bytes 110624 | tf_op jit(solution)/shard_map/ppermute | solution.py:28
  164.1 5.7 %collective-permute-done.21.refs_2_ = bf16[72,768]{1,0:T(8,128)(2,1)S(1)} collective-permute-done((bf16[72,768]{1,0:T(8,128)(2,1)S(1)}, bf16[72,768]{1,0:T(8,128)(2,1)S(1)}, u32[]{:S(2)}, u32[]{:S(2)}) %collective-permute-start.21) | collective-permute-done | bytes 110624 | tf_op jit(solution)/shard_map/ppermute | solution.py:28
  169.8 0.5 shard_map.96
  170.3 0.7 collective-permute-start.23
  171.0 6.0 %collective-permute-start.24 = (bf16[128,768]{1,0:T(8,128)(2,1)S(1)}, bf16[128,768]{1,0:T(8,128)(2,1)S(1)}, u32[]{:S(2)}, u32[]{:S(2)}) collective-permute-start(bf16[128,768]{1,0:T(8,128)(2,1)S(1)} %collective-permute-done.23.refs_0_), channel_id=1, source_target_pairs={{0,1},{1,2},{2,3},{3,4},{4,5},{5,6},{6,7},{7,0},{8,9},{9,10},{10,1... | collective-permute-start | bytes 589832 | tf_op jit(solution)/shard_map/ppermute | solution.py:40
  177.0 17.1 %collective-permute-start.25 = (bf16[128,768]{1,0:T(8,128)(2,1)S(1)}, bf16[128,768]{1,0:T(8,128)(2,1)S(1)}, u32[]{:S(2)}, u32[]{:S(2)}) collective-permute-start(bf16[128,768]{1,0:T(8,128)(2,1)S(1)} %collective-permute-done.23.refs_0_), channel_id=1, source_target_pairs={{0,7},{1,0},{2,1},{3,2},{4,3},{5,4},{6,5},{7,6},{8,15},{9,8},{10,9... | collective-permute-start | bytes 589832 | tf_op jit(solution)/shard_map/ppermute | solution.py:40
  194.1 5.1 %collective-permute-done.24.refs_1_ = bf16[128,768]{1,0:T(8,128)(2,1)S(1)} collective-permute-done((bf16[128,768]{1,0:T(8,128)(2,1)S(1)}, bf16[128,768]{1,0:T(8,128)(2,1)S(1)}, u32[]{:S(2)}, u32[]{:S(2)}) %collective-permute-start.24) | collective-permute-done | bytes 196640 | tf_op jit(solution)/shard_map/ppermute | solution.py:40
  199.3 0.1 stack.203
  199.4 3.3 %collective-permute-start.27 = (bf16[128,768]{1,0:T(8,128)(2,1)S(1)}, bf16[128,768]{1,0:T(8,128)(2,1)S(1)}, u32[]{:S(2)}, u32[]{:S(2)}) collective-permute-start(bf16[128,768]{1,0:T(8,128)(2,1)S(1)} %collective-permute-done.25.refs_2_), channel_id=1, source_target_pairs={{0,7},{1,0},{2,1},{3,2},{4,3},{5,4},{6,5},{7,6},{8,15},{9,8},{10,9... | collective-permute-start | bytes 589832 | tf_op jit(solution)/shard_map/ppermute | solution.py:40
  202.7 5.0 %collective-permute-done.26.refs_3_ = bf16[128,768]{1,0:T(8,128)(2,1)S(1)} collective-permute-done((bf16[128,768]{1,0:T(8,128)(2,1)S(1)}, bf16[128,768]{1,0:T(8,128)(2,1)S(1)}, u32[]{:S(2)}, u32[]{:S(2)}) %collective-permute-start.26) | collective-permute-done | bytes 196640 | tf_op jit(solution)/shard_map/ppermute | solution.py:40
  207.7 0.1 stack.161.slab_ref
  207.8 3.3 %collective-permute-start.29 = (bf16[128,768]{1,0:T(8,128)(2,1)S(1)}, bf16[128,768]{1,0:T(8,128)(2,1)S(1)}, u32[]{:S(2)}, u32[]{:S(2)}) collective-permute-start(bf16[128,768]{1,0:T(8,128)(2,1)S(1)} %collective-permute-done.27.refs_4_), channel_id=1, source_target_pairs={{0,7},{1,0},{2,1},{3,2},{4,3},{5,4},{6,5},{7,6},{8,15},{9,8},{10,9... | collective-permute-start | bytes 589832 | tf_op jit(solution)/shard_map/ppermute | solution.py:40
  211.1 4.3 %collective-permute-done.28.refs_5_ = bf16[128,768]{1,0:T(8,128)(2,1)S(1)} collective-permute-done((bf16[128,768]{1,0:T(8,128)(2,1)S(1)}, bf16[128,768]{1,0:T(8,128)(2,1)S(1)}, u32[]{:S(2)}, u32[]{:S(2)}) %collective-permute-start.28) | collective-permute-done | bytes 196640 | tf_op jit(solution)/shard_map/ppermute | solution.py:40
  215.4 4.5 %gather_fusion = bf16[32,72,768]{2,1,0:T(8,128)(2,1)} fusion(bf16[32,72,768]{2,1,0:T(8,128)(2,1)} %all-to-all-done, s32[1024]{0:T(1024)S(1)} %pad_clamp_fusion), kind=kCustom, calls=%fused_computation | custom fusion | bytes 7078016 | tf_op jit(solution)/shard_map/gather | solution.py:225
  219.9 8.6 %fusion.4 = bf16[768,1024]{1,0:T(8,128)(2,1)} fusion(bf16[2304,768]{1,0:T(8,128)(2,1)} %bitcast.78, bf16[2304,2048]{1,0:T(8,128)(2,1)} %get-tuple-element.14), kind=kOutput, calls=%fused_computation.5 | convolution fusion | flops 3624665088 | bytes 9830400 | tf_op jit(solution)/shard_map/dot_general | solution.py:227
  228.5 7.3 %fusion.7 = bf16[768,1024]{1,0:T(8,128)(2,1)} fusion(bf16[2304,768]{1,0:T(8,128)(2,1)S(1)} %bitcast.79, bf16[2304,2048]{1,0:T(8,128)(2,1)} %get-tuple-element.14), kind=kOutput, calls=%fused_computation.6 | convolution fusion | flops 3624665088 | bytes 9830400 | tf_op jit(solution)/shard_map/dot_general | solution.py:230
  235.8 1.8 shard_map.97
  (36 shorter events, 0.4 us)
Async XLA Ops:
  2.1 1.0 copy-start.1
  3.2 1.0 copy-start.2
  5.7 10.0 %collective-permute-start.1 = (bf16[72,2048]{1,0:T(8,128)(2,1)S(1)}, bf16[72,2048]{1,0:T(8,128)(2,1)S(1)}, u32[]{:S(2)}, u32[]{:S(2)}) collective-permute-start(bf16[72,2048]{1,0:T(8,128)(2,1)S(1)} %get-tuple-element.10), channel_id=1, source_target_pairs={{0,64},{8,72},{16,80},{24,88},{32,96},{40,104},{48,112},{56,120},{... | collective-permute-start | bytes 884744 | tf_op jit(solution)/shard_map/ppermute | solution.py:28
  7.9 11.3 %collective-permute-start.2 = (bf16[72,2048]{1,0:T(8,128)(2,1)S(1)}, bf16[72,2048]{1,0:T(8,128)(2,1)S(1)}, u32[]{:S(2)}, u32[]{:S(2)}) collective-permute-start(bf16[72,2048]{1,0:T(8,128)(2,1)S(1)} %get-tuple-element.11), channel_id=1, source_target_pairs={{0,128},{8,136},{16,144},{24,152},{32,160},{40,168},{48,176},{56,1... | collective-permute-start | bytes 884744 | tf_op jit(solution)/shard_map/ppermute | solution.py:28
  8.6 13.8 %collective-permute-start.3 = (bf16[72,2048]{1,0:T(8,128)(2,1)S(1)}, bf16[72,2048]{1,0:T(8,128)(2,1)S(1)}, u32[]{:S(2)}, u32[]{:S(2)}) collective-permute-start(bf16[72,2048]{1,0:T(8,128)(2,1)S(1)} %get-tuple-element.12), channel_id=1, source_target_pairs={{0,192},{8,200},{16,208},{24,216},{32,224},{40,232},{48,240},{56,2... | collective-permute-start | bytes 884744 | tf_op jit(solution)/shard_map/ppermute | solution.py:28
  23.1 29.5 %collective-permute-start.4 = (bf16[288,2048]{1,0:T(8,128)(2,1)}, bf16[288,2048]{1,0:T(8,128)(2,1)S(1)}, u32[]{:S(2)}, u32[]{:S(2)}) collective-permute-start(bf16[288,2048]{1,0:T(8,128)(2,1)} %constant_dynamic-update-slice_fusion.refs_0_), channel_id=1, source_target_pairs={{0,16},{8,24},{16,32},{24,40},{32,48},{40,56},{48,0},{56,8},{64,80... | collective-permute-start | bytes 3538952 | tf_op jit(solution)/shard_map/ppermute | solution.py:32
  24.8 28.2 %collective-permute-start.5 = (bf16[288,2048]{1,0:T(8,128)(2,1)}, bf16[288,2048]{1,0:T(8,128)(2,1)S(1)}, u32[]{:S(2)}, u32[]{:S(2)}) collective-permute-start(bf16[288,2048]{1,0:T(8,128)(2,1)} %constant_dynamic-update-slice_fusion.refs_0_), channel_id=1, source_target_pairs={{0,48},{8,56},{16,0},{24,8},{32,16},{40,24},{48,32},{56,40},{64,11... | collective-permute-start | bytes 3538952 | tf_op jit(solution)/shard_map/ppermute | solution.py:32
  26.4 43.2 %collective-permute-start.8 = (bf16[288,2048]{1,0:T(8,128)(2,1)}, bf16[288,2048]{1,0:T(8,128)(2,1)}, u32[]{:S(2)}, u32[]{:S(2)}) collective-permute-start(bf16[288,2048]{1,0:T(8,128)(2,1)} %constant_dynamic-update-slice_fusion.refs_0_), channel_id=1, source_target_pairs={{0,8},{8,0},{16,24},{24,16},{32,40},{40,32},{48,56},{56,48},{64,72... | collective-permute-start | bytes 3538952 | tf_op jit(solution)/shard_map/ppermute | solution.py:36
  52.7 15.9 %collective-permute-start.6 = (bf16[144,2048]{1,0:T(8,128)(2,1)S(1)}, bf16[144,2048]{1,0:T(8,128)(2,1)S(1)}, u32[]{:S(2)}, u32[]{:S(2)}) collective-permute-start(bf16[144,2048]{1,0:T(8,128)(2,1)S(1)} %slice.66), channel_id=1, source_target_pairs={{0,16},{8,24},{16,32},{24,40},{32,48},{40,56},{48,0},{56,8},{64,80... | collective-permute-start | bytes 1769480 | tf_op jit(solution)/shard_map/ppermute | solution.py:32
  53.0 16.5 %collective-permute-start.9 = (bf16[288,2048]{1,0:T(8,128)(2,1)S(1)}, bf16[288,2048]{1,0:T(8,128)(2,1)}, u32[]{:S(2)}, u32[]{:S(2)}) collective-permute-start(bf16[288,2048]{1,0:T(8,128)(2,1)S(1)} %collective-permute-done.4.refs_1_), channel_id=1, source_target_pairs={{0,8},{8,0},{16,24},{24,16},{32,40},{40,32},{48,56},{56,48},{64,72... | collective-permute-start | bytes 3538952 | tf_op jit(solution)/shard_map/ppermute | solution.py:36
  53.1 16.5 %collective-permute-start.10 = (bf16[288,2048]{1,0:T(8,128)(2,1)S(1)}, bf16[288,2048]{1,0:T(8,128)(2,1)}, u32[]{:S(2)}, u32[]{:S(2)}) collective-permute-start(bf16[288,2048]{1,0:T(8,128)(2,1)S(1)} %collective-permute-done.5.refs_2_), channel_id=1, source_target_pairs={{0,8},{8,0},{16,24},{24,16},{32,40},{40,32},{48,56},{56,48},{64,72... | collective-permute-start | bytes 3538952 | tf_op jit(solution)/shard_map/ppermute | solution.py:36
  53.7 15.8 %collective-permute-start.7 = (bf16[144,2048]{1,0:T(8,128)(2,1)S(1)}, bf16[144,2048]{1,0:T(8,128)(2,1)S(1)}, u32[]{:S(2)}, u32[]{:S(2)}) collective-permute-start(bf16[144,2048]{1,0:T(8,128)(2,1)S(1)} %slice.67), channel_id=1, source_target_pairs={{0,48},{8,56},{16,0},{24,8},{32,16},{40,24},{48,32},{56,40},{64,11... | collective-permute-start | bytes 1769480 | tf_op jit(solution)/shard_map/ppermute | solution.py:32
  68.5 2.1 collective-permute-start.11
  69.5 2.1 collective-permute-start.12
  92.1 18.9 %copy-start = (bf16[128,6144]{1,0:T(8,128)(2,1)S(1)}, bf16[128,6144]{1,0:T(8,128)(2,1)}, u32[]{:S(2)}) copy-start(bf16[128,6144]{1,0:T(8,128)(2,1)} %tok_ref.1) | copy-start | bytes 4718596
  93.4 16.4 %collective-permute-start.13 = (bf16[288,768]{1,0:T(8,128)(2,1)S(1)}, bf16[288,768]{1,0:T(8,128)(2,1)S(1)}, u32[]{:S(2)}, u32[]{:S(2)}) collective-permute-start(bf16[288,768]{1,0:T(8,128)(2,1)S(1)} %get-tuple-element.19), channel_id=1, source_target_pairs={{0,1},{1,2},{2,3},{3,4},{4,5},{5,6},{6,7},{7,0},{8,9},{9,10},{10,1... | collective-permute-start | bytes 1327112 | tf_op jit(solution)/shard_map/ppermute | solution.py:40
  95.4 26.6 %collective-permute-start.17 = (bf16[288,768]{1,0:T(8,128)(2,1)S(1)}, bf16[288,768]{1,0:T(8,128)(2,1)S(1)}, u32[]{:S(2)}, u32[]{:S(2)}) collective-permute-start(bf16[288,768]{1,0:T(8,128)(2,1)S(1)} %get-tuple-element.20), channel_id=1, source_target_pairs={{0,7},{1,0},{2,1},{3,2},{4,3},{5,4},{6,5},{7,6},{8,15},{9,8},{10,9... | collective-permute-start | bytes 1327112 | tf_op jit(solution)/shard_map/ppermute | solution.py:40
  110.9 13.0 %collective-permute-start.14 = (bf16[288,768]{1,0:T(8,128)(2,1)S(1)}, bf16[288,768]{1,0:T(8,128)(2,1)S(1)}, u32[]{:S(2)}, u32[]{:S(2)}) collective-permute-start(bf16[288,768]{1,0:T(8,128)(2,1)S(1)} %fusion.15), channel_id=1, source_target_pairs={{0,1},{1,2},{2,3},{3,4},{4,5},{5,6},{6,7},{7,0},{8,9},{9,10},{10,1... | collective-permute-start | bytes 1327112 | tf_op jit(solution)/shard_map/ppermute | solution.py:40
  114.1 101.3 %all-to-all-start = ((bf16[32,72,768]{2,1,0:T(8,128)(2,1)}), bf16[32,72,768]{2,1,0:T(8,128)(2,1)}, u32[]{:S(2)}, u32[]{:S(2)}) async-start(bf16[32,72,768]{2,1,0:T(8,128)(2,1)} %shard_map.98), calls=%async_computation | async-start | bytes 7077888 | tf_op jit(solution)/shard_map/all_to_all | solution.py:221
  125.3 12.1 %collective-permute-start.15 = (bf16[288,768]{1,0:T(8,128)(2,1)S(1)}, bf16[288,768]{1,0:T(8,128)(2,1)S(1)}, u32[]{:S(2)}, u32[]{:S(2)}) collective-permute-start(bf16[288,768]{1,0:T(8,128)(2,1)S(1)} %get-tuple-element.17), channel_id=1, source_target_pairs={{0,1},{1,2},{2,3},{3,4},{4,5},{5,6},{6,7},{7,0},{8,9},{9,10},{10,1... | collective-permute-start | bytes 1327112 | tf_op jit(solution)/shard_map/ppermute | solution.py:40
  125.4 12.0 %collective-permute-start.18 = (bf16[288,768]{1,0:T(8,128)(2,1)S(1)}, bf16[288,768]{1,0:T(8,128)(2,1)S(1)}, u32[]{:S(2)}, u32[]{:S(2)}) collective-permute-start(bf16[288,768]{1,0:T(8,128)(2,1)S(1)} %get-tuple-element.18), channel_id=1, source_target_pairs={{0,7},{1,0},{2,1},{3,2},{4,3},{5,4},{6,5},{7,6},{8,15},{9,8},{10,9... | collective-permute-start | bytes 1327112 | tf_op jit(solution)/shard_map/ppermute | solution.py:40
  138.7 12.1 %collective-permute-start.19 = (bf16[288,768]{1,0:T(8,128)(2,1)S(1)}, bf16[288,768]{1,0:T(8,128)(2,1)S(1)}, u32[]{:S(2)}, u32[]{:S(2)}) collective-permute-start(bf16[288,768]{1,0:T(8,128)(2,1)S(1)} %get-tuple-element.16), channel_id=1, source_target_pairs={{0,7},{1,0},{2,1},{3,2},{4,3},{5,4},{6,5},{7,6},{8,15},{9,8},{10,9... | collective-permute-start | bytes 1327112 | tf_op jit(solution)/shard_map/ppermute | solution.py:40
  141.7 11.0 %collective-permute-start.16 = (bf16[288,768]{1,0:T(8,128)(2,1)S(1)}, bf16[288,768]{1,0:T(8,128)(2,1)S(1)}, u32[]{:S(2)}, u32[]{:S(2)}) collective-permute-start(bf16[288,768]{1,0:T(8,128)(2,1)S(1)} %get-tuple-element.15), channel_id=1, source_target_pairs={{0,1},{1,2},{2,3},{3,4},{4,5},{5,6},{6,7},{7,0},{8,9},{9,10},{10,1... | collective-permute-start | bytes 1327112 | tf_op jit(solution)/shard_map/ppermute | solution.py:40
  154.0 10.1 %collective-permute-start.20 = (bf16[72,768]{1,0:T(8,128)(2,1)S(1)}, bf16[72,768]{1,0:T(8,128)(2,1)S(1)}, u32[]{:S(2)}, u32[]{:S(2)}) collective-permute-start(bf16[72,768]{1,0:T(8,128)(2,1)S(1)} %get-tuple-element.23), channel_id=1, source_target_pairs={{0,192},{8,200},{16,208},{24,216},{32,224},{40,232},{48,240},{56,2... | collective-permute-start | bytes 331784 | tf_op jit(solution)/shard_map/ppermute | solution.py:28
  155.6 14.1 %collective-permute-start.21 = (bf16[72,768]{1,0:T(8,128)(2,1)S(1)}, bf16[72,768]{1,0:T(8,128)(2,1)S(1)}, u32[]{:S(2)}, u32[]{:S(2)}) collective-permute-start(bf16[72,768]{1,0:T(8,128)(2,1)S(1)} %get-tuple-element.22), channel_id=1, source_target_pairs={{0,128},{8,136},{16,144},{24,152},{32,160},{40,168},{48,176},{56,1... | collective-permute-start | bytes 331784 | tf_op jit(solution)/shard_map/ppermute | solution.py:28
  156.1 13.7 %collective-permute-start.22 = (bf16[72,768]{1,0:T(8,128)(2,1)S(1)}, bf16[72,768]{1,0:T(8,128)(2,1)S(1)}, u32[]{:S(2)}, u32[]{:S(2)}) collective-permute-start(bf16[72,768]{1,0:T(8,128)(2,1)S(1)} %get-tuple-element.21), channel_id=1, source_target_pairs={{0,64},{8,72},{16,80},{24,88},{32,96},{40,104},{48,112},{56,120},{... | collective-permute-start | bytes 331784 | tf_op jit(solution)/shard_map/ppermute | solution.py:28
  158.4 0.7 collective-permute-start
  170.3 0.7 collective-permute-start.23
  171.0 28.3 %collective-permute-start.24 = (bf16[128,768]{1,0:T(8,128)(2,1)S(1)}, bf16[128,768]{1,0:T(8,128)(2,1)S(1)}, u32[]{:S(2)}, u32[]{:S(2)}) collective-permute-start(bf16[128,768]{1,0:T(8,128)(2,1)S(1)} %collective-permute-done.23.refs_0_), channel_id=1, source_target_pairs={{0,1},{1,2},{2,3},{3,4},{4,5},{5,6},{6,7},{7,0},{8,9},{9,10},{10,1... | collective-permute-start | bytes 589832 | tf_op jit(solution)/shard_map/ppermute | solution.py:40
  177.0 22.4 %collective-permute-start.25 = (bf16[128,768]{1,0:T(8,128)(2,1)S(1)}, bf16[128,768]{1,0:T(8,128)(2,1)S(1)}, u32[]{:S(2)}, u32[]{:S(2)}) collective-permute-start(bf16[128,768]{1,0:T(8,128)(2,1)S(1)} %collective-permute-done.23.refs_0_), channel_id=1, source_target_pairs={{0,7},{1,0},{2,1},{3,2},{4,3},{5,4},{6,5},{7,6},{8,15},{9,8},{10,9... | collective-permute-start | bytes 589832 | tf_op jit(solution)/shard_map/ppermute | solution.py:40
  199.3 8.5 %collective-permute-start.26 = (bf16[128,768]{1,0:T(8,128)(2,1)S(1)}, bf16[128,768]{1,0:T(8,128)(2,1)S(1)}, u32[]{:S(2)}, u32[]{:S(2)}) collective-permute-start(bf16[128,768]{1,0:T(8,128)(2,1)S(1)} %collective-permute-done.24.refs_1_), channel_id=1, source_target_pairs={{0,1},{1,2},{2,3},{3,4},{4,5},{5,6},{6,7},{7,0},{8,9},{9,10},{10,1... | collective-permute-start | bytes 589832 | tf_op jit(solution)/shard_map/ppermute | solution.py:40
  199.4 8.4 %collective-permute-start.27 = (bf16[128,768]{1,0:T(8,128)(2,1)S(1)}, bf16[128,768]{1,0:T(8,128)(2,1)S(1)}, u32[]{:S(2)}, u32[]{:S(2)}) collective-permute-start(bf16[128,768]{1,0:T(8,128)(2,1)S(1)} %collective-permute-done.25.refs_2_), channel_id=1, source_target_pairs={{0,7},{1,0},{2,1},{3,2},{4,3},{5,4},{6,5},{7,6},{8,15},{9,8},{10,9... | collective-permute-start | bytes 589832 | tf_op jit(solution)/shard_map/ppermute | solution.py:40
  207.7 7.7 %collective-permute-start.28 = (bf16[128,768]{1,0:T(8,128)(2,1)S(1)}, bf16[128,768]{1,0:T(8,128)(2,1)S(1)}, u32[]{:S(2)}, u32[]{:S(2)}) collective-permute-start(bf16[128,768]{1,0:T(8,128)(2,1)S(1)} %collective-permute-done.26.refs_3_), channel_id=1, source_target_pairs={{0,1},{1,2},{2,3},{3,4},{4,5},{5,6},{6,7},{7,0},{8,9},{9,10},{10,1... | collective-permute-start | bytes 589832 | tf_op jit(solution)/shard_map/ppermute | solution.py:40
  207.8 28.0 %collective-permute-start.29 = (bf16[128,768]{1,0:T(8,128)(2,1)S(1)}, bf16[128,768]{1,0:T(8,128)(2,1)S(1)}, u32[]{:S(2)}, u32[]{:S(2)}) collective-permute-start(bf16[128,768]{1,0:T(8,128)(2,1)S(1)} %collective-permute-done.27.refs_4_), channel_id=1, source_target_pairs={{0,7},{1,0},{2,1},{3,2},{4,3},{5,4},{6,5},{7,6},{8,15},{9,8},{10,9... | collective-permute-start | bytes 589832 | tf_op jit(solution)/shard_map/ppermute | solution.py:40
  215.4 20.4 %collective-permute-start.30 = (bf16[128,768]{1,0:T(8,128)(2,1)S(1)}, bf16[128,768]{1,0:T(8,128)(2,1)S(1)}, u32[]{:S(2)}, u32[]{:S(2)}) collective-permute-start(bf16[128,768]{1,0:T(8,128)(2,1)S(1)} %collective-permute-done.28.refs_5_), channel_id=1, source_target_pairs={{0,1},{1,2},{2,3},{3,4},{4,5},{5,6},{6,7},{7,0},{8,9},{9,10},{10,1... | collective-permute-start | bytes 589832 | tf_op jit(solution)/shard_map/ppermute | solution.py:40
  219.9 8.6 %copy-start.3 = (bf16[32,72,768]{2,1,0:T(8,128)(2,1)S(1)}, bf16[32,72,768]{2,1,0:T(8,128)(2,1)}, u32[]{:S(2)}) copy-start(bf16[32,72,768]{2,1,0:T(8,128)(2,1)} %gather_fusion) | copy-start | bytes 10616836
